TPU v7x, 512 devices: a whole 4x4x16 slice. The times are simulated.
512 devices in a mesh: dp: 8 (over x, core), expert: 64 (over y, z).
Axes of the slice: x: 4, y: 4, z: 16, core: 2. Of those that a mesh axis runs over, the one named last changes fastest.
Arguments:
- tokens_in: bfloat16 [65536, 3584], P(('dp', 'expert')), may hold values from -6 to 6
- out_grad: bfloat16 [65536, 3584], P(('dp', 'expert')), may hold values from -0.59765625 to 0.59765625
- router_logits: float32 [65536, 192], P(('dp', 'expert')), may hold values from -12 to 250
- expert_ids: int32 [65536, 8], P(('dp', 'expert')), may hold values from 0 to 191, all different within a row; in each aligned block of 128 rows (0 to 127, 128 to 255, ...) at most 8 rows name the same one
- saved_hidden: bfloat16 [8, 64, 64, 8, 1024], P('dp', 'expert'), may hold values from -6 to 6
- down_weight: bfloat16 [64, 1024, 3584], P('expert', 'dp'), may hold values from -0.1875 to 0.1875
Outputs:
- hidden_grad: bfloat16 [8, 64, 64, 8, 1024], P('dp', 'expert')
- logit_grad: float32 [65536, 192], P(('dp', 'expert'))
- router_grad: float32 [3584, 192], P('expert', 'dp')
Inputs may be any that keep to these rules, and one draw needn't show every extreme that they name: `expert_ids`: among the 128 rows of one device no expert is named by more than 8 rows, a bound that some block reaches.
All inputs are finite; a program needn't handle non-finite values.
Results may differ from a plain program's by a relative error of at most 0.013.
Values may be sent and summed in bfloat16 or wider, within the bound.
A program may use at most 64 MiB of HBM per device.

v0:
```python
import jax
import jax.numpy as jnp
from jax import lax
from jax.sharding import PartitionSpec as P

RSCALE = 2.827
ZLOSS = 0.25


def entering(shard, axis, combine, identity):
    length, place = (lax.axis_size(axis), lax.axis_index(axis))
    everything = lax.all_gather(shard.astype(jnp.bfloat16), axis)
    start = jnp.broadcast_to(jnp.asarray(identity, shard.dtype), shard.shape)

    def lap(k, before):
        reached = k < place
        new = combine(before, everything[k].astype(shard.dtype))
        return jnp.where(reached, new, before)

    return lax.fori_loop(0, length, lap, start)


def from_root(value, axis, source):
    kept = jnp.where(lax.axis_index(axis) == source, value, 0).astype(value.dtype)
    return lax.psum(kept, axis)


def slot_table(ids_block, flight, cap):
    owners = jnp.arange(flight, dtype=jnp.int32)
    chosen = jnp.any(ids_block[:, :, None] == owners[None, None, :], axis=1)
    as_int = chosen.astype(jnp.int32)
    rank = jnp.cumsum(as_int, axis=0) - as_int
    places = jnp.arange(cap, dtype=jnp.int32)
    table = chosen[None, :, :] & (rank[None, :, :] == places[:, None, None])
    return jnp.transpose(table, (2, 0, 1))


def own_columns(panel):
    count = panel.shape[1] // lax.axis_size("dp")
    return lax.dynamic_slice_in_dim(panel, lax.axis_index("dp") * count, count, 1)


def local(tokens_in, out_grad, router_logits, expert_ids, saved_hidden, down_weight):
    highest = lax.Precision.HIGHEST
    flight = lax.axis_size("expert")
    cap = saved_hidden.shape[3]
    hidden = saved_hidden.shape[4]
    width = out_grad.shape[1]
    experts = router_logits.shape[1]
    top = jnp.max(router_logits, axis=1, keepdims=True)
    shifted = jnp.exp(router_logits - top)
    total = jnp.sum(shifted, axis=1, keepdims=True)
    probs = shifted / total
    lse = top + jnp.log(total)
    columns = jnp.arange(experts, dtype=jnp.int32)
    picks = (expert_ids[:, :, None] == columns[None, None, :]).astype(jnp.float32)
    chosen_logit = jnp.sum(picks * router_logits[:, None, :], axis=2)
    scores = jax.nn.sigmoid(chosen_logit)
    ssum = jnp.sum(scores, axis=1, keepdims=True)
    gates = RSCALE * scores / ssum
    gate_half = gates.astype(jnp.bfloat16)
    in_window = picks[:, :, :flight]
    gate_te = jnp.sum(in_window * gate_half.astype(jnp.float32)[:, :, None], axis=1)
    table = slot_table(expert_ids, flight, cap)
    table_half = table.astype(jnp.bfloat16)
    table_full = table.astype(jnp.float32)
    send_rows = jnp.einsum(
        "ect,td->ecd", table_half, out_grad, preferred_element_type=jnp.float32
    ).astype(jnp.bfloat16)
    send_gates = jnp.einsum("ect,te->ec", table_full, gate_te, precision=highest).astype(
        jnp.bfloat16
    )
    recv_rows, recv_gates = (
        lax.all_to_all(send_rows, "expert", split_axis=0, concat_axis=0, tiled=True),
        lax.all_to_all(send_gates, "expert", split_axis=0, concat_axis=0, tiled=True),
    )
    flat_rows = recv_rows.reshape(flight * cap, width)
    part = lax.dot_general(
        flat_rows,
        lax.all_gather(down_weight, "dp", axis=1, tiled=True)[0],
        (((1,), (1,)), ((), ())),
        preferred_element_type=jnp.float32,
    )
    slot_gates = recv_gates.reshape(flight * cap, 1).astype(jnp.float32)
    hidden_grad = (slot_gates * part).astype(jnp.bfloat16).reshape(1, 1, flight, cap, hidden)
    saved_flat = saved_hidden.reshape(flight * cap, hidden)
    gate_grad = jnp.sum(saved_flat * part, axis=1).reshape(flight, cap)
    returned = lax.all_to_all(gate_grad, "expert", split_axis=0, concat_axis=0, tiled=True)
    grad_te = jnp.einsum("ect,ec->te", table_full, returned, precision=highest)
    grad_choice = jnp.sum(in_window * grad_te[:, None, :], axis=2)
    mixed = jnp.sum(grad_choice * gates, axis=1, keepdims=True) / RSCALE
    dscore = RSCALE / ssum * (grad_choice - mixed)
    dchosen = dscore * scores * (1.0 - scores)
    logit_grad = jnp.sum(picks * dchosen[:, :, None], axis=1) + 2.0 * ZLOSS * lse * probs
    tokens_full = tokens_in.astype(jnp.float32)
    own_rows = lax.psum_scatter(
        lax.dot_general(tokens_full, logit_grad, (((0,), (0,)), ((), ())), precision=highest),
        "expert",
        scatter_dimension=0,
        tiled=True,
    )
    before = entering(
        own_rows, "dp", lambda earlier, later: earlier + later, jnp.zeros_like(own_rows)
    )
    finished = before + own_rows
    spread = from_root(finished.astype(jnp.bfloat16), "dp", lax.axis_size("dp") - 1).astype(
        finished.dtype
    )
    router_grad = own_columns(spread)
    return (hidden_grad, logit_grad, router_grad)


def solution(mesh):
    in_specs = (
        P(("dp", "expert"), None),
        P(("dp", "expert"), None),
        P(("dp", "expert"), None),
        P(("dp", "expert"), None),
        P("dp", "expert", None, None, None),
        P("expert", "dp", None),
    )
    out_specs = (P("dp", "expert", None, None, None), P(("dp", "expert"), None), P("expert", "dp"))
    return jax.shard_map(local, mesh=mesh, in_specs=in_specs, out_specs=out_specs, check_vma=False)
```

profile of v0, /device:TPU:8, one launch (start us, length us, event | category | flops | bytes accessed | tf_op | source)
XLA Modules:
  0.0 974.6 jit_solution(7703707765535747499)
XLA Ops:
  7.2 0.8 fusion.6
  8.5 3.0 convolution_convert_fusion
  11.5 19.0 %all-to-all-start.1 = ((bf16[64,8,3584]{2,1,0:T(8,128)(2,1)}), bf16[64,8,3584]{2,1,0:T(8,128)(2,1)}, u32[]{:S(2)}, u32[]{:S(2)}) async-start(bf16[64,8,3584]{2,1,0:T(8,128)(2,1)} %convolution_convert_fusion), calls=%async_computation.1 | async-start | bytes 7340032 | tf_op jit(solution)/shard_map/all_to_all | solution.py:74
  30.6 0.7 all-gather.3.cloned.1.call-update
  31.7 55.6 %all-gather.3.cloned.1.call-done = bf16[1,1024,3584]{2,1,0:T(8,128)(2,1)} async-done(((bf16[1,128,3584]{2,1,0:T(8,128)(2,1)}), bf16[1,1024,3584]{2,1,0:T(8,128)(2,1)}) %all-gather.3.cloned.1.call-update) | async-done | bytes 7340048 | tf_op jit(solution)/shard_map/all_gather | solution.py:80
  87.3 106.5 %all-to-all-done.1 = bf16[64,8,3584]{2,1,0:T(8,128)(2,1)} async-done(((bf16[64,8,3584]{2,1,0:T(8,128)(2,1)}), bf16[64,8,3584]{2,1,0:T(8,128)(2,1)}, u32[]{:S(2)}, u32[]{:S(2)}) %all-to-all-start.1) | async-done | bytes 3670048 | tf_op jit(solution)/shard_map/all_to_all | solution.py:74
  193.8 8.4 fusion.3
  202.2 0.7 all_to_all.20
  202.9 9.7 all-to-all-start.2
  212.7 13.4 %all-to-all-done.2 = f32[64,1,8]{2,1,0:T(1,128)S(1)} async-done(((f32[64,1,8]{2,1,0:T(1,128)}), f32[64,1,8]{2,1,0:T(1,128)S(1)}, u32[]{:S(2)}, u32[]{:S(2)}) %all-to-all-start.2) | async-done | bytes 2080 | tf_op jit(solution)/shard_map/all_to_all | solution.py:88
  226.1 0.4 fusion.8
  226.7 4.0 convolution_bitcast_fusion
  230.7 4.7 copy.61
  235.5 0.4 fusion.11
  235.9 0.7 copy.52
  236.6 5.5 all-to-all-start
  242.1 13.5 %all-to-all-done = bf16[64,1,8]{2,1,0:T(2,128)(2,1)S(1)} async-done(((bf16[64,1,8]{2,1,0:T(2,128)(2,1)}), bf16[64,1,8]{2,1,0:T(2,128)(2,1)S(1)}, u32[]{:S(2)}, u32[]{:S(2)}) %all-to-all-start) | async-done | bytes 1056 | tf_op jit(solution)/shard_map/all_to_all | solution.py:75
  255.9 1.2 fusion.4
  257.0 668.6 %reduce-scatter.4.cloned.1.call-done = f32[56,192]{1,0:T(8,128)} async-done(((f32[3584,192]{1,0:T(8,128)}), f32[56,192]{1,0:T(8,128)}) %reduce-scatter.4.cloned.1.call-update) | async-done | bytes 43024 | tf_op jit(solution)/shard_map/reduce_scatter | solution.py:96
  925.6 0.8 convert_element_type.90
  926.4 13.2 %all-gather = bf16[448,192]{1,0:T(8,128)(2,1)S(1)} all-gather(bf16[56,192]{1,0:T(8,128)(2,1)S(1)} %convert_element_type.90), channel_id=2, replica_groups=mesh['dp'=8,'expert'=64] {'dp'}, dimensions={0}, use_global_device_ids=true | all-gather | bytes 193536 | tf_op jit(solution)/shard_map/all_gather | solution.py:12
  940.1 0.9 copy.62
  941.0 26.1 %psum.7 = bf16[56,192]{0,1:T(8,128)(2,1)S(1)} all-reduce(bf16[56,192]{0,1:T(8,128)(2,1)S(1)} %fusion.20), channel_id=1, replica_groups=mesh['dp'=8,'expert'=64] {'dp'}, use_global_device_ids=true, to_apply=%region_14.15 | all-reduce | flops 10752 | bytes 43008 | tf_op jit(solution)/shard_map/psum | solution.py:25
  967.2 0.6 dynamic-slice_convert_fusion
  (46 shorter events, 2.0 us)
Async XLA Ops:
  7.2 1.3 copy-start
  11.5 19.8 %copy-start.1 = (f32[128,192]{0,1:T(8,128)S(1)}, f32[128,192]{0,1:T(8,128)}, u32[]{:S(2)}) copy-start(f32[128,192]{0,1:T(8,128)} %param.10) | copy-start | bytes 294916
  11.5 19.8 %copy-start.3 = (s32[128,8]{0,1:T(8,128)S(1)}, s32[128,8]{0,1:T(8,128)}, u32[]{:S(2)}) copy-start(s32[128,8]{0,1:T(8,128)} %param.11) | copy-start | bytes 12292
  11.5 182.3 %all-to-all-start.1 = ((bf16[64,8,3584]{2,1,0:T(8,128)(2,1)}), bf16[64,8,3584]{2,1,0:T(8,128)(2,1)}, u32[]{:S(2)}, u32[]{:S(2)}) async-start(bf16[64,8,3584]{2,1,0:T(8,128)(2,1)} %convolution_convert_fusion), calls=%async_computation.1 | async-start | bytes 7340032 | tf_op jit(solution)/shard_map/all_to_all | solution.py:74
  30.6 56.7 %all-gather.3.cloned.1.call-start = ((), (), s32[]{:S(2)}) async-start(), calls=%async_computation.4 | async-start | bytes 8257536 | tf_op jit(solution)/shard_map/all_gather | solution.py:80
  202.9 23.1 %all-to-all-start.2 = ((f32[64,1,8]{2,1,0:T(1,128)}), f32[64,1,8]{2,1,0:T(1,128)S(1)}, u32[]{:S(2)}, u32[]{:S(2)}) async-start(f32[64,1,8]{2,1,0:T(1,128)} %bitcast.12), calls=%async_computation.2 | async-start | bytes 65536 | tf_op jit(solution)/shard_map/all_to_all | solution.py:88
  212.6 713.0 %reduce-scatter.4.cloned.1.call-start = ((), (), s32[]{:S(2)}) async-start(), calls=%async_computation.5 | async-start | bytes 3727360 | tf_op jit(solution)/shard_map/reduce_scatter | solution.py:96
  226.7 8.7 copy-start.2
  236.6 19.0 %all-to-all-start = ((bf16[64,1,8]{2,1,0:T(2,128)(2,1)}), bf16[64,1,8]{2,1,0:T(2,128)(2,1)S(1)}, u32[]{:S(2)}, u32[]{:S(2)}) async-start(bf16[64,1,8]{2,1,0:T(2,128)(2,1)} %copy.52), calls=%async_computation | async-start | bytes 65536 | tf_op jit(solution)/shard_map/all_to_all | solution.py:75
Sparse Core Ops, SparseCore 0:
  33.5 53.7 all-gather.2
  235.6 689.9 reduce-scatter.3
where the time goes:
time: 975 us
  waiting for transfers between devices  858 us (88%)
  blocking collectives  39.4 us (4%)
  starting transfers between devices  34.3 us (4%)
  matrix products  16.1 us (2%)
  between operations  14.2 us (1%)
    reduce_scatter x1, waiting for transfers between devices, local(): lax.psum_scatter(lax.dot_general(tokens_full, logit_grad, (((0,), (0,)),...  669 us
    all_to_all x1, waiting for transfers between devices, local(): lax.all_to_all(send_rows, 'expert', split_axis=0, concat_axis=0, tiled=True)  107 us
    all_gather x1, waiting for transfers between devices, local(): lax.all_gather(down_weight, 'dp', axis=1, tiled=True)[0]  55.6 us
    psum x1, blocking collectives, from_root(): return lax.psum(kept, axis)  26.1 us
  transfers between devices with their start and end apart: 5, of which 5 were waited for; matrix products, arithmetic and copies ran while one was open for 0% of the time, Pallas kernels for 0%

commit v1 on v0

--- a/solution.py
+++ b/solution.py
@@ -77,7 +77,9 @@
     flat_rows = recv_rows.reshape(flight * cap, width)
     part = lax.dot_general(
         flat_rows,
-        lax.all_gather(down_weight, "dp", axis=1, tiled=True)[0],
+        jnp.concatenate(
+            lax.all_to_all(jnp.stack([down_weight] * lax.axis_size("dp")), "dp", 0, 0), axis=1
+        )[0],
         (((1,), (1,)), ((), ())),
         preferred_element_type=jnp.float32,
     )

time: 975 us -> 1060 us (1.087)
  the two profiles are of different devices: /device:TPU:8 before, /device:TPU:64 now
where the time goes in v1:
time: 1060 us
  waiting for transfers between devices  936 us (88%)
  blocking collectives  39.4 us (4%)
  starting transfers between devices  39.1 us (4%)
  matrix products  16 us (2%)
  between operations  14.2 us (1%)
  local copies, waits for them, and re-layouts  12.6 us (1%)
    reduce_scatter x1, waiting for transfers between devices, local(): lax.psum_scatter(lax.dot_general(tokens_full, logit_grad, (((0,), (0,)),...  668 us
    all_to_all x1, waiting for transfers between devices, local(): lax.all_to_all(send_rows, 'expert', split_axis=0, concat_axis=0, tiled=True)  163 us
    all_to_all x1, waiting for transfers between devices, local(): lax.all_to_all(jnp.stack([down_weight] * lax.axis_size('dp')), 'dp', 0, 0)  79.9 us
    psum x1, blocking collectives, from_root(): return lax.psum(kept, axis)  26.3 us
  transfers between devices with their start and end apart: 5, of which 5 were waited for; matrix products, arithmetic and copies ran while one was open for 1% of the time, Pallas kernels for 0%

profile of v1, /device:TPU:64, one launch (start us, length us, event | category | flops | bytes accessed | tf_op | source)
XLA Modules:
  0.0 1061.0 jit_solution(16227078849551884136)
XLA Ops:
  7.2 4.9 stack.2
  12.1 5.0 all-to-all-start.2
  17.6 2.9 convolution_convert_fusion
  20.5 79.9 %all-to-all-done.2 = bf16[8,1,128,3584]{3,2,1,0:T(8,128)(2,1)} async-done(((bf16[8,1,128,3584]{3,2,1,0:T(8,128)(2,1)}), bf16[8,1,128,3584]{3,2,1,0:T(8,128)(2,1)}, u32[]{:S(2)}, u32[]{:S(2)}) %all-to-all-start.2) | async-done | bytes 7340064 | tf_op jit(solution)/shard_map/all_to_all | solution.py:81
  100.4 18.1 %all-to-all-start.1 = ((bf16[64,8,3584]{2,1,0:T(8,128)(2,1)}), bf16[64,8,3584]{2,1,0:T(8,128)(2,1)}, u32[]{:S(2)}, u32[]{:S(2)}) async-start(bf16[64,8,3584]{2,1,0:T(8,128)(2,1)} %convolution_convert_fusion), calls=%async_computation.1 | async-start | bytes 7340032 | tf_op jit(solution)/shard_map/all_to_all | solution.py:74
  118.9 162.8 %all-to-all-done.1 = bf16[64,8,3584]{2,1,0:T(8,128)(2,1)} async-done(((bf16[64,8,3584]{2,1,0:T(8,128)(2,1)}), bf16[64,8,3584]{2,1,0:T(8,128)(2,1)}, u32[]{:S(2)}, u32[]{:S(2)}) %all-to-all-start.1) | async-done | bytes 3670048 | tf_op jit(solution)/shard_map/all_to_all | solution.py:74
  281.7 8.4 fusion.2
  290.1 0.7 all_to_all.24
  290.8 9.6 all-to-all-start.3
  300.5 12.5 %all-to-all-done.3 = f32[64,1,8]{2,1,0:T(1,128)S(1)} async-done(((f32[64,1,8]{2,1,0:T(1,128)}), f32[64,1,8]{2,1,0:T(1,128)S(1)}, u32[]{:S(2)}, u32[]{:S(2)}) %all-to-all-start.3) | async-done | bytes 2080 | tf_op jit(solution)/shard_map/all_to_all | solution.py:90
  313.0 0.4 fusion.7
  313.6 4.0 convolution_bitcast_fusion
  317.6 4.7 copy.61
  322.3 0.4 fusion.10
  322.8 0.7 copy.52
  323.5 6.3 all-to-all-start
  329.9 12.6 %all-to-all-done = bf16[64,1,8]{2,1,0:T(2,128)(2,1)S(1)} async-done(((bf16[64,1,8]{2,1,0:T(2,128)(2,1)}), bf16[64,1,8]{2,1,0:T(2,128)(2,1)S(1)}, u32[]{:S(2)}, u32[]{:S(2)}) %all-to-all-start) | async-done | bytes 1056 | tf_op jit(solution)/shard_map/all_to_all | solution.py:75
  342.7 1.2 fusion.3
  343.8 668.1 %reduce-scatter.4.cloned.1.call-done = f32[56,192]{1,0:T(8,128)} async-done(((f32[3584,192]{1,0:T(8,128)}), f32[56,192]{1,0:T(8,128)}) %reduce-scatter.4.cloned.1.call-update) | async-done | bytes 43024 | tf_op jit(solution)/shard_map/reduce_scatter | solution.py:98
  1011.9 0.8 convert_element_type.90
  1012.7 13.2 %all-gather = bf16[448,192]{1,0:T(8,128)(2,1)S(1)} all-gather(bf16[56,192]{1,0:T(8,128)(2,1)S(1)} %convert_element_type.90), channel_id=2, replica_groups=mesh['dp'=8,'expert'=64] {'dp'}, dimensions={0}, use_global_device_ids=true | all-gather | bytes 193536 | tf_op jit(solution)/shard_map/all_gather | solution.py:12
  1026.3 0.9 copy.62
  1027.3 26.3 %psum.7 = bf16[56,192]{0,1:T(8,128)(2,1)S(1)} all-reduce(bf16[56,192]{0,1:T(8,128)(2,1)S(1)} %fusion.19), channel_id=1, replica_groups=mesh['dp'=8,'expert'=64] {'dp'}, use_global_device_ids=true, to_apply=%region_14.15 | all-reduce | flops 10752 | bytes 43008 | tf_op jit(solution)/shard_map/psum | solution.py:25
  1053.5 0.6 dynamic-slice_convert_fusion
  (46 shorter events, 2.0 us)
Async XLA Ops:
  7.2 10.5 copy-start
  12.1 5.0 copy-start.3
  12.1 88.4 %all-to-all-start.2 = ((bf16[8,1,128,3584]{3,2,1,0:T(8,128)(2,1)}), bf16[8,1,128,3584]{3,2,1,0:T(8,128)(2,1)}, u32[]{:S(2)}, u32[]{:S(2)}) async-start(bf16[8,1,128,3584]{3,2,1,0:T(8,128)(2,1)} %stack.2), calls=%async_computation.2 | async-start | bytes 14680064 | tf_op jit(solution)/shard_map/all_to_all | solution.py:81
  20.5 98.0 %copy-start.1 = (f32[128,192]{0,1:T(8,128)S(1)}, f32[128,192]{0,1:T(8,128)}, u32[]{:S(2)}) copy-start(f32[128,192]{0,1:T(8,128)} %param.10) | copy-start | bytes 294916
  100.4 181.2 %all-to-all-start.1 = ((bf16[64,8,3584]{2,1,0:T(8,128)(2,1)}), bf16[64,8,3584]{2,1,0:T(8,128)(2,1)}, u32[]{:S(2)}, u32[]{:S(2)}) async-start(bf16[64,8,3584]{2,1,0:T(8,128)(2,1)} %convolution_convert_fusion), calls=%async_computation.1 | async-start | bytes 7340032 | tf_op jit(solution)/shard_map/all_to_all | solution.py:74
  290.8 22.2 %all-to-all-start.3 = ((f32[64,1,8]{2,1,0:T(1,128)}), f32[64,1,8]{2,1,0:T(1,128)S(1)}, u32[]{:S(2)}, u32[]{:S(2)}) async-start(f32[64,1,8]{2,1,0:T(1,128)} %bitcast.13), calls=%async_computation.3 | async-start | bytes 65536 | tf_op jit(solution)/shard_map/all_to_all | solution.py:90
  300.5 711.4 %reduce-scatter.4.cloned.1.call-start = ((), (), s32[]{:S(2)}) async-start(), calls=%async_computation.5 | async-start | bytes 3727360 | tf_op jit(solution)/shard_map/reduce_scatter | solution.py:98
  313.6 8.7 copy-start.2
  323.5 19.0 %all-to-all-start = ((bf16[64,1,8]{2,1,0:T(2,128)(2,1)}), bf16[64,1,8]{2,1,0:T(2,128)(2,1)S(1)}, u32[]{:S(2)}, u32[]{:S(2)}) async-start(bf16[64,1,8]{2,1,0:T(2,128)(2,1)} %copy.52), calls=%async_computation | async-start | bytes 65536 | tf_op jit(solution)/shard_map/all_to_all | solution.py:75
Sparse Core Ops, SparseCore 0:
  322.5 689.3 reduce-scatter.3
